TPU v7x, 32 devices: a whole 2x2x4 slice. The times are simulated.
32 devices in a mesh: dp: 4 (over y, x), context: 8 (over z, core).
Axes of the slice: x: 2, y: 2, z: 4, core: 2. Of those that a mesh axis runs over, the one named last changes fastest.
Arguments:
- queries: bfloat16 [4, 1024, 2048], P('dp', 'context'), may hold values from -6 to 6
- keys: bfloat16 [4, 1024, 2048], P('dp', 'context'), may hold values from -6 to 6
- values: bfloat16 [4, 1024, 2048], P('dp', 'context'), may hold values from -40 to 40
- gain: float32 [2048], replicated, may hold values from 0.1 to 1.9
- out_grad: bfloat16 [4, 1024, 2048], P('dp', 'context'), may hold values from -6 to 6
Outputs:
- query_grad: bfloat16 [4, 1024, 2048], P('dp', 'context')
- key_grad: bfloat16 [4, 1024, 2048], P('dp', 'context')
- value_grad: bfloat16 [4, 1024, 2048], P('dp', 'context')
- scale_factor_sensitivity: float32 [2048], replicated
All inputs are finite; a program needn't handle non-finite values.
Results may differ from a plain program's by a relative error of at most 0.0067.
Values may be sent and summed in bfloat16 or wider, within the bound.
A program may use at most 64 MiB of HBM per device.

v0:
```python
import jax
import jax.numpy as jnp
from jax import lax
from jax.sharding import PartitionSpec as P

HEADS = 16
HEAD_DIM = 128


def cumulative_total(block, backward):
    zeros = jnp.zeros_like(block[:, :1])
    if backward:
        after = jnp.flip(jnp.cumsum(jnp.flip(block, 1), axis=1), 1)
        return jnp.concatenate([after[:, 1:], zeros], axis=1)
    before = jnp.cumsum(block, axis=1)
    return jnp.concatenate([zeros, before[:, :-1]], axis=1)


def earlier_states(within_block_part):
    parts = lax.axis_size("context")
    spread = within_block_part.reshape(parts, 1, -1)
    summed = cumulative_total(
        lax.all_to_all(spread, "context", split_axis=0, concat_axis=1, tiled=True), False
    ).astype(jnp.bfloat16)
    result = lax.all_to_all(summed, "context", split_axis=1, concat_axis=0, tiled=True)
    return result.reshape(within_block_part.shape)


def later_grads(addend_piece):
    parts = lax.axis_size("context")
    spread = addend_piece.reshape(parts, 1, -1)
    summed = cumulative_total(
        lax.all_to_all(spread, "context", split_axis=0, concat_axis=1, tiled=True), True
    ).astype(jnp.bfloat16)
    result = lax.all_to_all(summed, "context", split_axis=1, concat_axis=0, tiled=True)
    return result.reshape(addend_piece.shape)


def shards(queries, keys, values, gain, out_grad):
    count = queries.shape[1]
    width = queries.shape[2]
    probe_vectors = queries[0].reshape(count, HEADS, HEAD_DIM)
    key_matrix = keys[0].reshape(count, HEADS, HEAD_DIM)
    payload_table = values[0].reshape(count, HEADS, HEAD_DIM)
    grad_rows = out_grad[0].reshape(count, HEADS, HEAD_DIM)
    within_block_part = jnp.einsum(
        "ogd,ogt->gdt", key_matrix, payload_table, preferred_element_type=jnp.float32
    )
    earlier_memory_tile = earlier_states(within_block_part)
    rows = lax.broadcasted_iota(jnp.int32, (count, count), 0)
    cols = lax.broadcasted_iota(jnp.int32, (count, count), 1)
    causal = (rows >= cols)[None]
    scores = jnp.einsum(
        "chk,shk->hcs", probe_vectors, key_matrix, preferred_element_type=jnp.float32
    )
    attn = jnp.where(causal, scores, 0.0).astype(jnp.bfloat16)
    unnormed_output = jnp.einsum(
        "arf,rfc->arc", probe_vectors, earlier_memory_tile, preferred_element_type=jnp.float32
    )
    unnormed_output = unnormed_output + jnp.einsum(
        "hcs,shv->chv", attn, payload_table, preferred_element_type=jnp.float32
    )
    rms = jnp.sqrt(jnp.mean(unnormed_output * unnormed_output, axis=-1, keepdims=True) + 1e-06)
    unit = unnormed_output / rms
    grad_float = grad_rows.astype(jnp.float32)
    gain_part = jnp.sum(grad_float * unit, axis=0).reshape(width)
    scaled = gain.reshape(1, HEADS, HEAD_DIM) * grad_float
    normed_output_grad = (
        (scaled - unit * jnp.mean(scaled * unit, axis=-1, keepdims=True)) / rms
    ).astype(jnp.bfloat16)
    addend_piece = jnp.einsum(
        "ogd,ogt->gdt", probe_vectors, normed_output_grad, preferred_element_type=jnp.float32
    )
    suffix_state_block = later_grads(addend_piece)
    dscores = jnp.einsum(
        "chv,shv->hcs", normed_output_grad, payload_table, preferred_element_type=jnp.float32
    )
    dattn = jnp.where(causal, dscores, 0.0).astype(jnp.bfloat16)
    probe_sensitivity = jnp.einsum(
        "djy,joy->djo", normed_output_grad, earlier_memory_tile, preferred_element_type=jnp.float32
    )
    probe_sensitivity = probe_sensitivity + jnp.einsum(
        "hcs,shk->chk", dattn, key_matrix, preferred_element_type=jnp.float32
    )
    key_derivative = jnp.einsum(
        "hcs,chk->shk", dattn, probe_vectors, preferred_element_type=jnp.float32
    )
    key_derivative = key_derivative + jnp.einsum(
        "qwe,wge->qwg", payload_table, suffix_state_block, preferred_element_type=jnp.float32
    )
    payload_sensitivity = jnp.einsum(
        "hcs,chv->shv", attn, normed_output_grad, preferred_element_type=jnp.float32
    )
    payload_sensitivity = payload_sensitivity + jnp.einsum(
        "wzt,ztm->wzm", key_matrix, suffix_state_block, preferred_element_type=jnp.float32
    )
    total = lax.psum(gain_part, ("dp", "context"))
    tokens_all = queries.shape[0] * lax.axis_size("dp") * count * lax.axis_size("context")
    scale_factor_sensitivity = total / jnp.sqrt(jnp.float32(tokens_all))
    shape = (1, count, width)
    return (
        probe_sensitivity.reshape(shape).astype(jnp.bfloat16),
        key_derivative.reshape(shape).astype(jnp.bfloat16),
        payload_sensitivity.reshape(shape).astype(jnp.bfloat16),
        scale_factor_sensitivity,
    )


def solution(mesh):
    return jax.shard_map(
        shards,
        mesh=mesh,
        in_specs=(
            P("dp", "context", None),
            P("dp", "context", None),
            P("dp", "context", None),
            P(),
            P("dp", "context", None),
        ),
        out_specs=(
            P("dp", "context", None),
            P("dp", "context", None),
            P("dp", "context", None),
            P(),
        ),
        check_vma=False,
    )
```

profile of v0, /device:TPU:0, one launch (start us, length us, event | category | flops | bytes accessed | tf_op | source)
XLA Modules:
  0.0 183.8 jit_solution(2268961454433209915)
XLA Ops:
  0.6 1.1 copy.100
  1.8 0.5 copy.73
  2.3 0.6 copy-done.7
  3.4 32.7 %all_to_all.42 = f32[8,1,32768]{2,1,0:T(1,128)S(1)} all-to-all(f32[8,1,32768]{2,1,0:T(1,128)S(1)} %bitcast.84), channel_id=1, replica_groups=mesh['dp'=4,'context'=8] {'context'}, dimensions={0} | all-to-all | bytes 2097152 | tf_op jit(solution)/shard_map/all_to_all | solution.py:23
  36.1 0.7 fusion.8
  36.8 0.9 slice.17
  37.8 1.0 pad_bitcast_fusion.1
  38.8 0.5 broadcast.31
  39.3 3.8 %reduce.4 = bf16[8,32768]{1,0:T(8,128)(2,1)S(1)} reduce(bf16[8,1,32768]{2,1,0:T(2,128)(2,1)S(1)} %pad_bitcast_fusion.1, bf16[]{:T(256)} %broadcast.31), dimensions={1}, to_apply=%pad_bitcast_fusion.1.reduce_sub_computation | reduce | bytes 1048578
  43.1 1.2 reshape.110
  44.3 3.8 %all-to-all-start.1 = ((bf16[8,2,16384]{2,1,0:T(2,128)(2,1)}), bf16[8,2,16384]{2,1,0:T(2,128)(2,1)S(1)}, u32[]{:S(2)}, u32[]{:S(2)}) async-start(bf16[8,2,16384]{2,1,0:T(2,128)(2,1)} %reshape.110), calls=%async_computation.1 | async-start | bytes 1048576 | tf_op jit(solution)/shard_map/all_to_all | solution.py:25
  48.2 1.2 copy.76
  49.5 1.3 fusion.3
  50.8 12.4 %all-to-all-done.1 = bf16[8,2,16384]{2,1,0:T(2,128)(2,1)S(1)} async-done(((bf16[8,2,16384]{2,1,0:T(2,128)(2,1)}), bf16[8,2,16384]{2,1,0:T(2,128)(2,1)S(1)}, u32[]{:S(2)}, u32[]{:S(2)}) %all-to-all-start.1) | async-done | bytes 524320 | tf_op jit(solution)/shard_map/all_to_all | solution.py:25
  63.2 1.8 reshape.111
  65.0 5.0 %bitcast_reduce_fusion.1 = bf16[8,32768]{1,0:T(8,128)(2,1)} fusion(bf16[8,1,32768]{2,1,0:T(2,128)(2,1)} %reshape.111), kind=kLoop, calls=%fused_computation.43 | loop fusion | bytes 1048576 | tf_op jit(solution)/shard_map/all_to_all | solution.py:25
  70.0 1.3 reshape.103
  71.3 0.5 convolution_bitcast_fusion.6
  72.5 0.5 multiply_reduce_fusion.2
  73.1 0.7 copy-done.9
  73.8 0.7 multiply_reduce_fusion
  75.2 1.3 copy.88
  76.5 4.6 %all-to-all-start.2 = ((f32[8,1,32768]{2,1,0:T(1,128)}), f32[8,1,32768]{2,1,0:T(1,128)}, u32[]{:S(2)}, u32[]{:S(2)}) async-start(f32[8,1,32768]{2,1,0:T(1,128)} %bitcast.83), calls=%async_computation.2 | async-start | bytes 2097152 | tf_op jit(solution)/shard_map/all_to_all | solution.py:33
  81.1 1.3 convolution_bitcast_fusion.4
  82.4 25.1 %all-to-all-done.2 = f32[8,1,32768]{2,1,0:T(1,128)} async-done(((f32[8,1,32768]{2,1,0:T(1,128)}), f32[8,1,32768]{2,1,0:T(1,128)}, u32[]{:S(2)}, u32[]{:S(2)}) %all-to-all-start.2) | async-done | bytes 1048608 | tf_op jit(solution)/shard_map/all_to_all | solution.py:33
  107.5 1.3 rev.5
  108.8 0.7 fusion.21
  109.5 0.9 slice.14
  110.5 1.9 %slice.18 = bf16[1,7,32768]{2,0,1:T(2,128)(2,1)} reverse(bf16[1,7,32768]{2,0,1:T(2,128)(2,1)S(1)} %slice.14), dimensions={1} | reverse | bytes 917504 | tf_op jit(solution)/shard_map/slice | solution.py:14
  112.4 2.2 %pad_bitcast_fusion = bf16[8,1,32768]{2,1,0:T(2,128)(2,1)S(1)} fusion(bf16[1,7,32768]{2,0,1:T(2,128)(2,1)} %slice.18), kind=kLoop, calls=%fused_computation.44 | loop fusion | bytes 983040
  114.6 4.6 %reduce.5 = bf16[8,32768]{1,0:T(8,128)(2,1)} reduce(bf16[8,1,32768]{2,1,0:T(2,128)(2,1)S(1)} %pad_bitcast_fusion, bf16[]{:T(256)} %broadcast.31), dimensions={1}, to_apply=%pad_bitcast_fusion.reduce_sub_computation | reduce | bytes 1048578
  119.2 2.2 %reshape.112 = bf16[8,2,16384]{2,1,0:T(2,128)(2,1)} reshape(bf16[8,32768]{1,0:T(8,128)(2,1)} %reduce.5) | data formatting | bytes 1048576
  121.4 4.1 %all-to-all-start.3 = ((bf16[8,2,16384]{2,1,0:T(2,128)(2,1)}), bf16[8,2,16384]{2,1,0:T(2,128)(2,1)}, u32[]{:S(2)}, u32[]{:S(2)}) async-start(bf16[8,2,16384]{2,1,0:T(2,128)(2,1)} %reshape.112), calls=%async_computation.3 | async-start | bytes 1048576 | tf_op jit(solution)/shard_map/all_to_all | solution.py:35
  125.6 0.5 fusion.4
  126.1 0.5 copy-done.1
  127.0 0.5 fusion.5
  127.4 1.0 copy.93
  128.5 41.0 %psum.7 = f32[2048]{0:T(1024)S(1)} all-reduce(f32[2048]{0:T(1024)S(1)} %bitcast.93), channel_id=1, replica_groups=mesh['dp'=4,'context'=8] {'dp','context'}, use_global_device_ids=true, to_apply=%region_5.6 | all-reduce | flops 2048 | bytes 16384 | tf_op jit(solution)/shard_map/psum | solution.py:97
  169.4 0.6 broadcast_multiply_fusion
  170.0 2.3 %fusion.22 = f32[16,128,128]{2,1,0:T(8,128)} fusion(bf16[128,16,128]{0,2,1:T(8,128)(2,1)S(1)} %divide_convert_fusion, bf16[16,128,128]{2,1,0:T(8,128)(2,1)} %fusion.3), kind=kOutput, calls=%fused_computation.47 | convolution fusion | flops 67108864 | bytes 2097152 | tf_op jit(solution)/shard_map/hcs,chv->shv/dot_general | solution.py:91
  172.4 2.2 %reshape.113 = bf16[8,1,32768]{2,1,0:T(2,128)(2,1)S(1)} reshape(bf16[8,2,16384]{2,1,0:T(2,128)(2,1)} %all-to-all-done.3) | data formatting | bytes 1048576
  174.6 3.8 %bitcast_reduce_fusion = bf16[8,32768]{1,0:T(8,128)(2,1)} fusion(bf16[8,1,32768]{2,1,0:T(2,128)(2,1)S(1)} %reshape.113), kind=kLoop, calls=%fused_computation.42 | loop fusion | bytes 1048576 | tf_op jit(solution)/shard_map/all_to_all | solution.py:35
  178.4 1.3 reshape.105
  179.6 0.5 convolution_bitcast_fusion.1
  180.1 0.7 copy-done.5
  180.9 0.5 fusion.6
  181.7 1.0 copy.94
  182.8 1.0 copy.95
  (26 shorter events, 2.8 us)
Async XLA Ops:
  1.8 1.0 copy-start.7
  2.3 0.8 copy-start
  44.3 3.8 %copy-start.8 = (bf16[1,128,2048]{2,1,0:T(8,128)(2,1)S(1)}, bf16[1,128,2048]{2,1,0:T(8,128)(2,1)}, u32[]{:S(2)}) copy-start(bf16[1,128,2048]{2,1,0:T(8,128)(2,1)} %param.5) | copy-start | bytes 1572868
  44.3 18.9 %all-to-all-start.1 = ((bf16[8,2,16384]{2,1,0:T(2,128)(2,1)}), bf16[8,2,16384]{2,1,0:T(2,128)(2,1)S(1)}, u32[]{:S(2)}, u32[]{:S(2)}) async-start(bf16[8,2,16384]{2,1,0:T(2,128)(2,1)} %reshape.110), calls=%async_computation.1 | async-start | bytes 1048576 | tf_op jit(solution)/shard_map/all_to_all | solution.py:25
  71.3 0.8 copy-start.2
  71.3 1.2 copy-start.6
  73.1 0.7 copy-start.9
  76.5 4.6 %copy-start.3 = (bf16[16,128,128]{2,1,0:T(8,128)(2,1)S(1)}, bf16[16,128,128]{2,1,0:T(8,128)(2,1)}, u32[]{:S(2)}) copy-start(bf16[16,128,128]{2,1,0:T(8,128)(2,1)} %copy-done.2) | copy-start | bytes 1572868
  76.5 31.0 %all-to-all-start.2 = ((f32[8,1,32768]{2,1,0:T(1,128)}), f32[8,1,32768]{2,1,0:T(1,128)}, u32[]{:S(2)}, u32[]{:S(2)}) async-start(f32[8,1,32768]{2,1,0:T(1,128)} %bitcast.83), calls=%async_computation.2 | async-start | bytes 2097152 | tf_op jit(solution)/shard_map/all_to_all | solution.py:33
  121.4 50.9 %all-to-all-start.3 = ((bf16[8,2,16384]{2,1,0:T(2,128)(2,1)}), bf16[8,2,16384]{2,1,0:T(2,128)(2,1)}, u32[]{:S(2)}, u32[]{:S(2)}) async-start(bf16[8,2,16384]{2,1,0:T(2,128)(2,1)} %reshape.112), calls=%async_computation.3 | async-start | bytes 1048576 | tf_op jit(solution)/shard_map/all_to_all | solution.py:35
  125.6 1.0 copy-start.1
  125.6 1.4 copy-start.4
  179.6 1.2 copy-start.5
where the time goes:
time: 185 us; the launch traced here: 184 us
  blocking collectives  73.7 us (40%)
  local copies, waits for them, and re-layouts  38.7 us (21%)
  waiting for transfers between devices  37.5 us (20%)
  starting transfers between devices  12.5 us (7%)
  other arithmetic  11.6 us (6%)
  matrix products  8.86 us (5%)
    psum x1, blocking collectives, shards(): total = lax.psum(gain_part, ('dp', 'context'))  41 us
    all_to_all x1, blocking collectives, earlier_states(): lax.all_to_all(spread, 'context', split_axis=0, concat_axis=1, tiled=True)  32.7 us
    all_to_all x1, waiting for transfers between devices, later_grads(): lax.all_to_all(spread, 'context', split_axis=0, concat_axis=1, tiled=True)  25.1 us
    unnamed x33, local copies, waits for them, and re-layouts  19.2 us
    all_to_all x1, waiting for transfers between devices, earlier_states(): lax.all_to_all(summed, 'context', split_axis=1, concat_axis=0, tiled=True)  12.4 us
    unnamed x2, other arithmetic  8.42 us
    all_to_all x1, local copies, waits for them, and re-layouts, earlier_states(): lax.all_to_all(summed, 'context', split_axis=1, concat_axis=0, tiled=True)  5.02 us
    all_to_all x1, starting transfers between devices, later_grads(): lax.all_to_all(spread, 'context', split_axis=0, concat_axis=1, tiled=True)  4.59 us
  transfers between devices with their start and end apart: 3, of which 2 were waited for; matrix products, arithmetic and copies ran while one was open for 5% of the time, Pallas kernels for 0%

commit v1 on v0

v1 whole, which is shorter than its diff:
```python
import functools
import math

import jax
import jax.numpy as jnp
from jax import lax
from jax.experimental import pallas as pl
from jax.experimental.pallas import tpu as pltpu
from jax.sharding import PartitionSpec as P

HEADS = 16
HALF = HEADS // 2
DIM = 128
F32 = jnp.float32
BF16 = jnp.bfloat16
MESH = pl.DeviceIdType.MESH


def nn(a, b):
    return lax.dot_general(a, b, (((1,), (0,)), ((), ())), preferred_element_type=F32)


def nt(a, b):
    return lax.dot_general(a, b, (((1,), (1,)), ((), ())), preferred_element_type=F32)


def tn(a, b):
    return lax.dot_general(a, b, (((0,), (0,)), ((), ())), preferred_element_type=F32)


def kernel(
    n_dp, n_ctx, tokens, link_t,
    q_ref, k_ref, v_ref, gain_ref, dy_ref,
    qg_ref, kg_ref, vg_ref, sg_ref,
    loc, xs, xr, ps, pr, fs, pre, attn, du, term, ts, tr, rs, rr, ss, suf, kp, vp,
    gloc, g1, g2, gout,
    x_sem, p_sem, f_sem, t_sem, r_sem, s_sem, g1s, g1r, g2s, g2r, g3s, g3r,
):
    dp = lax.axis_index("dp")
    ctx = lax.axis_index("context")
    chips = n_ctx // 2
    last = chips - 1
    z = ctx // 2
    core = ctx % 2
    sib = z * 2 + (1 - core)
    own0 = core * HALF
    sib0 = (1 - core) * HALF
    per = gout.shape[1]
    n_own = gout.shape[0]

    barrier = pltpu.get_barrier_semaphore()

    @pl.loop(0, n_ctx)
    def _(c):
        @pl.when(c != ctx)
        def _():
            pl.semaphore_signal(barrier, inc=1, device_id={"context": c}, device_id_type=MESH)

    @pl.loop(0, n_dp)
    def _(d):
        @pl.when(d != dp)
        def _():
            pl.semaphore_signal(barrier, inc=1, device_id={"dp": d}, device_id_type=MESH)

    def lanes(h):
        return pl.ds(pl.multiple_of(h * DIM, DIM), DIM)

    def remote(src, dst, sems, i, device):
        return pltpu.make_async_remote_copy(
            src_ref=src, dst_ref=dst, send_sem=sems.at[0, i], recv_sem=sems.at[1, i],
            device_id={"context": device}, device_id_type=MESH,
        )

    def swap_local(t):
        return remote(xs.at[t], xr.at[t], x_sem, t, sib)

    def pass_prefix(t):
        return remote(ps.at[t], pr.at[t], p_sem, t, jnp.minimum(ctx + 2, n_ctx - 2 + core))

    def give_prefix(t):
        return remote(fs.at[t], pre.at[own0 + t], f_sem, t, sib)

    def swap_term(t):
        return remote(ts.at[t], tr.at[t], t_sem, t, sib)

    def pass_suffix(t):
        return remote(rs.at[t], rr.at[t], r_sem, t, jnp.maximum(ctx - 2, core))

    def give_suffix(t):
        return remote(ss.at[t], suf.at[own0 + t], s_sem, t, sib)

    @pl.loop(0, HALF // 2)
    def _(i):
        for j in range(2):
            t = i * 2 + j
            s = lanes(sib0 + t)
            xs[t] = tn(k_ref[:, s], v_ref[:, s]).astype(BF16)

    pl.semaphore_wait(barrier, n_ctx - 1 + n_dp - 1)

    @pl.loop(0, HALF)
    def _(t):
        swap_local(t).start()

    @pl.loop(0, HALF // 2)
    def _(i):
        for j in range(2):
            t = i * 2 + j
            s = lanes(own0 + t)
            loc[t] = tn(k_ref[:, s], v_ref[:, s])

    @pl.when(z == 0)
    def _():
        pr[...] = jnp.zeros_like(pr)

    @pl.when(z == last)
    def _():
        rr[...] = jnp.zeros_like(rr)

    def prefix_chain(t):
        swap_local(t).wait_recv()

        @pl.when(z > 0)
        def _():
            pass_prefix(t).wait_recv()

        before = pr[t].astype(F32)
        other = xr[t].astype(F32)
        mine = loc[t]

        @pl.when(z < last)
        def _():
            ps[t] = (before + (mine + other)).astype(link_t)
            pass_prefix(t).start()

        @pl.when(core == 0)
        def _():
            fs[t] = (before + mine).astype(BF16)
            give_prefix(t).start()
            pre[own0 + t] = before.astype(BF16)

        @pl.when(core == 1)
        def _():
            fs[t] = before.astype(BF16)
            give_prefix(t).start()
            pre[own0 + t] = (before + other).astype(BF16)

    @pl.when(z == 0)
    def _():
        @pl.loop(0, HALF)
        def _(t):
            prefix_chain(t)

    rows = lax.broadcasted_iota(jnp.int32, (DIM, DIM), 0)
    cols = lax.broadcasted_iota(jnp.int32, (DIM, DIM), 1)

    @pl.loop(0, HEADS // 4)
    def _(i):
        for j in range(4):
            h = i * 4 + j
            s = lanes(h)
            attn[h] = jnp.where(rows >= cols, nt(q_ref[:, s], k_ref[:, s]), 0.0).astype(BF16)

    def through_norm(h):
        s = lanes(h)
        u = nn(q_ref[:, s], pre[h]) + nn(attn[h], v_ref[:, s])
        inv = lax.rsqrt(jnp.mean(u * u, axis=-1, keepdims=True) + 1e-6)
        unit = u * inv
        grad = dy_ref[:, s].astype(F32)
        gloc[h] = jnp.sum(grad * unit, axis=0, keepdims=True)
        scaled = gain_ref[:, s] * grad
        d = (scaled - unit * jnp.mean(scaled * unit, axis=-1, keepdims=True)) * inv
        d = d.astype(BF16)
        du[h] = d
        return tn(q_ref[:, s], d)

    def norm_step(t):
        remote(fs.at[t], pre.at[sib0 + t], f_sem, t, sib).wait_recv()
        other = through_norm(sib0 + t)
        mine = through_norm(own0 + t)
        ts[t] = other.astype(BF16)
        swap_term(t).start()
        term[t] = mine

    def suffix_chain(t):
        swap_term(t).wait_recv()

        @pl.when(z < last)
        def _():
            pass_suffix(t).wait_recv()

        after = rr[t].astype(F32)
        other = tr[t].astype(F32)
        mine = term[t]

        @pl.when(z > 0)
        def _():
            rs[t] = (after + (mine + other)).astype(link_t)
            pass_suffix(t).start()

        @pl.when(core == 0)
        def _():
            ss[t] = after.astype(BF16)
            give_suffix(t).start()
            suf[own0 + t] = (after + other).astype(BF16)

        @pl.when(core == 1)
        def _():
            ss[t] = (after + mine).astype(BF16)
            give_suffix(t).start()
            suf[own0 + t] = after.astype(BF16)

    def within_block(h):
        s = lanes(h)
        d = du[h]
        da = jnp.where(rows >= cols, nt(d, v_ref[:, s]), 0.0).astype(BF16)
        qg_ref[:, s] = (nt(d, pre[h]) + nn(da, k_ref[:, s])).astype(BF16)
        kp[h] = tn(da, q_ref[:, s])
        vp[h] = tn(attn[h], d)

    def finish(h):
        s = lanes(h)
        kg_ref[:, s] = (kp[h] + nt(v_ref[:, s], suf[h])).astype(BF16)
        vg_ref[:, s] = (vp[h] + nn(k_ref[:, s], suf[h])).astype(BF16)

    def gain_copy(src, dst, send, recv, device):
        return pltpu.make_async_remote_copy(
            src_ref=src, dst_ref=dst, send_sem=send, recv_sem=recv,
            device_id=device, device_id_type=MESH,
        )

    def to_owner(o):
        return gain_copy(
            gloc.at[pl.ds(o * per, per)], g1.at[ctx], g1s.at[o], g1r.at[ctx], {"context": o})

    def across(d):
        return gain_copy(g2.at[dp], g2.at[dp], g2s.at[d], g2r.at[dp], {"dp": d})

    def to_all(c):
        return gain_copy(gout.at[ctx], gout.at[ctx], g3s.at[c], g3r.at[ctx], {"context": c})

    def others(n, me, f):
        @pl.loop(0, n)
        def _(i):
            @pl.when(i != me)
            def _():
                f(i)

    def gain_first():
        others(n_own, ctx, lambda o: to_owner(o).start())

        @pl.when(ctx < n_own)
        def _():
            g1[ctx] = gloc[pl.ds(ctx * per, per)]

    def gain_second():
        @pl.when(ctx < n_own)
        def _():
            others(n_ctx, ctx, lambda c: gain_copy(
                gloc.at[pl.ds(0, per)], g1.at[c], g1s.at[0], g1r.at[c], {"context": c}).wait_recv())
            g2[dp] = jnp.sum(g1[...], axis=0)
            others(n_dp, dp, lambda d: across(d).start())

    def gain_third():
        @pl.when(ctx < n_own)
        def _():
            others(n_dp, dp, lambda d: gain_copy(
                g2.at[d], g2.at[d], g2s.at[d], g2r.at[d], {"dp": d}).wait_recv())
            gout[ctx] = jnp.sum(g2[...], axis=0) / jnp.sqrt(F32(tokens))
            others(n_ctx, ctx, lambda c: to_all(c).start())

    chain_lag = jnp.minimum(2 + HALF * (last - z), 2 * HALF + 1)
    finish_lag = jnp.maximum(chain_lag, HALF + 1) + 1

    @pl.loop(0, 3 * HALF + 2)
    def _(t):
        @pl.when((t < HALF) & (z > 0))
        def _():
            prefix_chain(t)

        @pl.when((t >= 1) & (t < HALF + 1))
        def _():
            norm_step(t - 1)

        @pl.when(t == HALF)
        def _():
            gain_first()

        c = t - chain_lag

        @pl.when((c >= 0) & (c < HALF))
        def _():
            suffix_chain(c)

        @pl.when(c == HALF - 1)
        def _():
            gain_second()

        w = t - (HALF + 1)

        @pl.when((w >= 0) & (w < HALF))
        def _():
            within_block(own0 + w)
            within_block(sib0 + w)

        f = t - finish_lag

        @pl.when((f >= 0) & (f < HALF))
        def _():
            remote(ss.at[f], suf.at[sib0 + f], s_sem, f, sib).wait_recv()
            finish(own0 + f)
            finish(sib0 + f)

    gain_third()
    others(n_own, ctx, lambda o: gain_copy(
        gout.at[o], gout.at[o], g3s.at[o], g3r.at[o], {"context": o}).wait_recv())
    for h in range(HEADS):
        sg_ref[:, h * DIM:(h + 1) * DIM] = gout[h // per, h % per]

    @pl.loop(0, HALF)
    def _(t):
        swap_local(t).wait_send()
        give_prefix(t).wait_send()
        swap_term(t).wait_send()
        give_suffix(t).wait_send()

        @pl.when(z < last)
        def _():
            pass_prefix(t).wait_send()

        @pl.when(z > 0)
        def _():
            pass_suffix(t).wait_send()

    others(n_own, ctx, lambda o: to_owner(o).wait_send())

    @pl.when(ctx < n_own)
    def _():
        others(n_dp, dp, lambda d: across(d).wait_send())
        others(n_ctx, ctx, lambda c: to_all(c).wait_send())


def shards(n_dp, n_ctx, queries, keys, values, gain, out_grad):
    count, width = queries.shape[1:]
    tokens = queries.shape[0] * n_dp * count * n_ctx
    link_t = BF16 if n_ctx <= 16 else F32
    n_own = min(n_ctx, HEADS)
    per = HEADS // n_own
    flat = lambda x: x.reshape(count, width)
    tile = lambda n, t: pltpu.VMEM((n, DIM, DIM), t)
    vmem = pl.BlockSpec(memory_space=pltpu.VMEM)
    dma = pltpu.SemaphoreType.DMA
    outs = pl.pallas_call(
        functools.partial(kernel, n_dp, n_ctx, tokens, link_t),
        out_shape=[jax.ShapeDtypeStruct((count, width), BF16)] * 3
        + [jax.ShapeDtypeStruct((1, width), F32)],
        in_specs=[vmem] * 5,
        out_specs=[vmem] * 4,
        scratch_shapes=[
            tile(HALF, F32), tile(HALF, BF16), tile(HALF, BF16),
            tile(HALF, link_t), tile(HALF, link_t), tile(HALF, BF16), tile(HEADS, BF16),
            tile(HEADS, BF16), tile(HEADS, BF16),
            tile(HALF, F32), tile(HALF, BF16), tile(HALF, BF16),
            tile(HALF, link_t), tile(HALF, link_t), tile(HALF, BF16), tile(HEADS, BF16),
            tile(HEADS, F32), tile(HEADS, F32),
            pltpu.VMEM((HEADS, 1, DIM), F32),
            pltpu.VMEM((n_ctx, per, 1, DIM), F32),
            pltpu.VMEM((n_dp, per, 1, DIM), F32),
            pltpu.VMEM((n_own, per, 1, DIM), F32),
        ]
        + [dma((2, HALF))] * 6
        + [dma((n_own,)), dma((n_ctx,)), dma((n_dp,)), dma((n_dp,)), dma((n_ctx,)), dma((n_own,))],
        compiler_params=pltpu.CompilerParams(
            collective_id=0, has_side_effects=True, vmem_limit_bytes=40 * 2**20),
        cost_estimate=pl.CostEstimate(
            flops=24 * HEADS * DIM**3, bytes_accessed=7 * 2 * count * width,
            transcendentals=HEADS * DIM),
    )(flat(queries), flat(keys), flat(values), gain.reshape(1, width), flat(out_grad))
    shape = (1, count, width)
    return (outs[0].reshape(shape), outs[1].reshape(shape), outs[2].reshape(shape),
            outs[3].reshape(width))


def solution(mesh):
    rows = P("dp", "context", None)
    return jax.shard_map(
        functools.partial(shards, mesh.shape["dp"], mesh.shape["context"]),
        mesh=mesh,
        in_specs=(rows, rows, rows, P(), rows),
        out_specs=(rows, rows, rows, P()),
        check_vma=False,
    )
```

time: 185 us -> 48.4 us (0.26)
  blocking collectives: 73.7 us -> 0 us
  Pallas kernels: 0 us -> 39.6 us
  waiting for transfers between devices: 37.5 us -> 0 us
  local copies, waits for them, and re-layouts: 38.7 us -> 7.83 us
  starting transfers between devices: 12.5 us -> 0 us
  other arithmetic: 11.6 us -> 0 us
  matrix products: 8.86 us -> 0 us
    psum x1 -> x0, blocking collectives: 41 us -> none  [shards(): total = lax.psum(gain_part, ('dp', 'context'))]
    pallas_call x0 -> x1, Pallas kernels: none -> 39.6 us  [shards(): pl.pallas_call(functools.partial(kernel, n_dp, n_ctx, tokens, link_t), ou...]
    all_to_all x3 -> x0, waiting for transfers between devices: 37.5 us -> none  [the longest x1 25.1 us: later_grads(): lax.all_to_all(spread, 'context', split_axis=0, concat_axis=1, tiled=True)]
    all_to_all x1 -> x0, blocking collectives: 32.7 us -> none  [earlier_states(): lax.all_to_all(spread, 'context', split_axis=0, concat_axis=1, tiled=True)]
    all_to_all x3 -> x0, starting transfers between devices: 12.5 us -> none  [the longest x1 4.59 us: later_grads(): lax.all_to_all(spread, 'context', split_axis=0, concat_axis=1, tiled=True)]
    unnamed x33 -> x14, local copies, waits for them, and re-layouts: 19.2 us -> 7.83 us
    dot_general x12 -> x0, matrix products: 8.86 us -> none  [the longest x1 2.32 us: shards(): jnp.einsum('hcs,chv->shv', attn, normed_output_grad, preferred_element_ty...]
    all_to_all x2 -> x0, local copies, waits for them, and re-layouts: 8.79 us -> none  [the longest x1 5.02 us: earlier_states(): lax.all_to_all(summed, 'context', split_axis=1, concat_axis=0, tiled=True)]
  transfers between devices with their start and end apart: 3 -> 0, of which waited for: 2 -> 0; matrix products, arithmetic and copies ran while one was open for 5% -> 0% of each run, Pallas kernels for 0% -> 0%
where the time goes in v1:
time: 48.4 us; the launch traced here: 48 us
  Pallas kernels  39.6 us (82%)
  local copies, waits for them, and re-layouts  7.83 us (16%)
  between operations  0.65 us (1%)
    pallas_call x1, Pallas kernels, shards(): pl.pallas_call(functools.partial(kernel, n_dp, n_ctx, tokens, link_t), ou...  39.6 us
    unnamed x14, local copies, waits for them, and re-layouts  7.83 us

profile of v1, /device:TPU:0, one launch (start us, length us, event | category | flops | bytes accessed | tf_op | source)
XLA Modules:
  0.0 48.0 jit_solution(17149231892891016509)
XLA Ops:
  0.6 0.0 copy-start.4
  0.6 0.7 %copy-done.4 = f32[2048]{0:T(1024)S(1)} copy-done((f32[2048]{0:T(1024)S(1)}, f32[2048]{0:T(1024)}, u32[]{:S(2)}) %copy-start.4) | copy-done | bytes 8216
  1.3 0.0 copy-start
  1.3 1.0 %copy-done = bf16[1,128,2048]{2,1,0:T(8,128)(2,1)S(1)} copy-done((bf16[1,128,2048]{2,1,0:T(8,128)(2,1)S(1)}, bf16[1,128,2048]{2,1,0:T(8,128)(2,1)}, u32[]{:S(2)}) %copy-start) | copy-done | bytes 524312
  2.4 0.0 copy-start.1
  2.4 1.0 %copy-done.1 = bf16[1,128,2048]{2,1,0:T(8,128)(2,1)S(1)} copy-done((bf16[1,128,2048]{2,1,0:T(8,128)(2,1)S(1)}, bf16[1,128,2048]{2,1,0:T(8,128)(2,1)}, u32[]{:S(2)}) %copy-start.1) | copy-done | bytes 524312
  3.4 0.0 copy-start.2
  3.4 1.0 %copy-done.2 = bf16[1,128,2048]{2,1,0:T(8,128)(2,1)S(1)} copy-done((bf16[1,128,2048]{2,1,0:T(8,128)(2,1)S(1)}, bf16[1,128,2048]{2,1,0:T(8,128)(2,1)}, u32[]{:S(2)}) %copy-start.2) | copy-done | bytes 524312
  4.5 0.0 copy-start.3
  4.5 1.0 %copy-done.3 = bf16[1,128,2048]{2,1,0:T(8,128)(2,1)S(1)} copy-done((bf16[1,128,2048]{2,1,0:T(8,128)(2,1)S(1)}, bf16[1,128,2048]{2,1,0:T(8,128)(2,1)}, u32[]{:S(2)}) %copy-start.3) | copy-done | bytes 524312
  5.5 39.6 %shard_map.84 = (bf16[128,2048]{1,0:T(8,128)(2,1)S(1)}, bf16[128,2048]{1,0:T(8,128)(2,1)S(1)}, bf16[128,2048]{1,0:T(8,128)(2,1)S(1)}, f32[1,2048]{1,0:T(1,128)S(1)}) custom-call(bf16[128,2048]{1,0:T(8,128)(2,1)S(1)} %bitcast.13, bf16[128,2048]{1,0:T(8,128)(2,1)S(1)} %bitcast.14, bf16[128,2048]{1,0:T(8,128)(2,1)S(1)} %bitcast.15, f32[1,2048]{1,0:T(1,128)S(1)} %bitcast.17, ...), custom_call_target="tpu_custom_call" | custom-call | flops 805306368 | bytes 3670016 | tf_op jit(solution)/shard_map/pallas_call | solution.py:353
  45.1 0.8 %copy.13 = bf16[1,128,2048]{2,1,0:T(8,128)(2,1)} copy(bf16[1,128,2048]{2,1,0:T(8,128)(2,1)S(1)} %bitcast.11) | data formatting | bytes 1048576
  45.9 0.8 %copy.14 = bf16[1,128,2048]{2,1,0:T(8,128)(2,1)} copy(bf16[1,128,2048]{2,1,0:T(8,128)(2,1)S(1)} %bitcast.10) | data formatting | bytes 1048576
  46.7 0.8 %copy.15 = bf16[1,128,2048]{2,1,0:T(8,128)(2,1)} copy(bf16[1,128,2048]{2,1,0:T(8,128)(2,1)S(1)} %bitcast.9) | data formatting | bytes 1048576
  47.4 0.6 %copy.16 = f32[2048]{0:T(1024)} copy(f32[2048]{0:T(1024)S(1)} %bitcast.12) | data formatting | bytes 16384
Async XLA Ops:
  0.6 0.7 %copy-start.4 = (f32[2048]{0:T(1024)S(1)}, f32[2048]{0:T(1024)}, u32[]{:S(2)}) copy-start(f32[2048]{0:T(1024)} %param.8) | copy-start | bytes 24580
  1.3 1.0 %copy-start = (bf16[1,128,2048]{2,1,0:T(8,128)(2,1)S(1)}, bf16[1,128,2048]{2,1,0:T(8,128)(2,1)}, u32[]{:S(2)}) copy-start(bf16[1,128,2048]{2,1,0:T(8,128)(2,1)} %param.5) | copy-start | bytes 1572868
  2.4 1.0 %copy-start.1 = (bf16[1,128,2048]{2,1,0:T(8,128)(2,1)S(1)}, bf16[1,128,2048]{2,1,0:T(8,128)(2,1)}, u32[]{:S(2)}) copy-start(bf16[1,128,2048]{2,1,0:T(8,128)(2,1)} %param.6) | copy-start | bytes 1572868
  3.4 1.0 %copy-start.2 = (bf16[1,128,2048]{2,1,0:T(8,128)(2,1)S(1)}, bf16[1,128,2048]{2,1,0:T(8,128)(2,1)}, u32[]{:S(2)}) copy-start(bf16[1,128,2048]{2,1,0:T(8,128)(2,1)} %param.7) | copy-start | bytes 1572868
  4.5 1.0 %copy-start.3 = (bf16[1,128,2048]{2,1,0:T(8,128)(2,1)S(1)}, bf16[1,128,2048]{2,1,0:T(8,128)(2,1)}, u32[]{:S(2)}) copy-start(bf16[1,128,2048]{2,1,0:T(8,128)(2,1)} %param.9) | copy-start | bytes 1572868

commit v2 on v1

--- a/solution.py
+++ b/solution.py
@@ -10,6 +10,11 @@
 
 HEADS = 16
 HALF = HEADS // 2
+WIDE = 1
+PARTS = HALF // WIDE
+NORM_LAG = 1
+CHAIN_LAG = 1
+FINISH_LAG = 1
 DIM = 128
 F32 = jnp.float32
 BF16 = jnp.bfloat16
@@ -30,11 +35,12 @@
 
 def kernel(
     n_dp, n_ctx, tokens, link_t,
-    q_ref, k_ref, v_ref, gain_ref, dy_ref,
-    qg_ref, kg_ref, vg_ref, sg_ref,
+    q_hbm, k_hbm, v_hbm, gain_hbm, dy_hbm,
+    qg_hbm, kg_hbm, vg_hbm, sg_hbm,
+    q_ref, k_ref, v_ref, gain_ref, dy_ref, qg_ref, kg_ref, vg_ref, sg_ref,
     loc, xs, xr, ps, pr, fs, pre, attn, du, term, ts, tr, rs, rr, ss, suf, kp, vp,
     gloc, g1, g2, gout,
-    x_sem, p_sem, f_sem, t_sem, r_sem, s_sem, g1s, g1r, g2s, g2r, g3s, g3r,
+    x_sem, p_sem, f_sem, t_sem, r_sem, s_sem, g1s, g1r, g2s, g2r, g3s, g3r, in_sem, out_sem,
 ):
     dp = lax.axis_index("dp")
     ctx = lax.axis_index("context")
@@ -48,6 +54,23 @@
     per = gout.shape[1]
     n_own = gout.shape[0]
 
+    def lanes(h):
+        return pl.ds(pl.multiple_of(h * DIM, DIM), DIM)
+
+    def half(h):
+        return pl.ds(pl.multiple_of(h * DIM, DIM), HALF * DIM)
+
+    sh, oh = half(sib0), half(own0)
+    loads = [
+        pltpu.make_async_copy(src, dst, in_sem.at[i])
+        for i, (src, dst) in enumerate([
+            (k_hbm.at[:, sh], k_ref.at[:, sh]), (v_hbm.at[:, sh], v_ref.at[:, sh]),
+            (k_hbm.at[:, oh], k_ref.at[:, oh]), (v_hbm.at[:, oh], v_ref.at[:, oh]),
+            (q_hbm, q_ref), (dy_hbm, dy_ref), (gain_hbm, gain_ref)])
+    ]
+    for load in loads:
+        load.start()
+
     barrier = pltpu.get_barrier_semaphore()
 
     @pl.loop(0, n_ctx)
@@ -62,8 +85,8 @@
         def _():
             pl.semaphore_signal(barrier, inc=1, device_id={"dp": d}, device_id_type=MESH)
 
-    def lanes(h):
-        return pl.ds(pl.multiple_of(h * DIM, DIM), DIM)
+    def part(t, base=0):
+        return pl.ds(base + t * WIDE, WIDE)
 
     def remote(src, dst, sems, i, device):
         return pltpu.make_async_remote_copy(
@@ -72,40 +95,46 @@
         )
 
     def swap_local(t):
-        return remote(xs.at[t], xr.at[t], x_sem, t, sib)
+        return remote(xs.at[part(t)], xr.at[part(t)], x_sem, t, sib)
 
     def pass_prefix(t):
-        return remote(ps.at[t], pr.at[t], p_sem, t, jnp.minimum(ctx + 2, n_ctx - 2 + core))
+        return remote(ps.at[part(t)], pr.at[part(t)], p_sem, t, jnp.minimum(ctx + 2, n_ctx - 2 + core))
 
     def give_prefix(t):
-        return remote(fs.at[t], pre.at[own0 + t], f_sem, t, sib)
+        return remote(fs.at[part(t)], pre.at[part(t, own0)], f_sem, t, sib)
 
     def swap_term(t):
-        return remote(ts.at[t], tr.at[t], t_sem, t, sib)
+        return remote(ts.at[part(t)], tr.at[part(t)], t_sem, t, sib)
 
     def pass_suffix(t):
-        return remote(rs.at[t], rr.at[t], r_sem, t, jnp.maximum(ctx - 2, core))
+        return remote(rs.at[part(t)], rr.at[part(t)], r_sem, t, jnp.maximum(ctx - 2, core))
 
     def give_suffix(t):
-        return remote(ss.at[t], suf.at[own0 + t], s_sem, t, sib)
-
-    @pl.loop(0, HALF // 2)
+        return remote(ss.at[part(t)], suf.at[part(t, own0)], s_sem, t, sib)
+
+    loads[0].wait()
+    loads[1].wait()
+
+    @pl.loop(0, HALF // 4)
     def _(i):
-        for j in range(2):
-            t = i * 2 + j
+        for j in range(4):
+            t = i * 4 + j
             s = lanes(sib0 + t)
             xs[t] = tn(k_ref[:, s], v_ref[:, s]).astype(BF16)
 
     pl.semaphore_wait(barrier, n_ctx - 1 + n_dp - 1)
 
-    @pl.loop(0, HALF)
+    @pl.loop(0, PARTS)
     def _(t):
         swap_local(t).start()
 
-    @pl.loop(0, HALF // 2)
+    loads[2].wait()
+    loads[3].wait()
+
+    @pl.loop(0, HALF // 4)
     def _(i):
-        for j in range(2):
-            t = i * 2 + j
+        for j in range(4):
+            t = i * 4 + j
             s = lanes(own0 + t)
             loc[t] = tn(k_ref[:, s], v_ref[:, s])
 
@@ -124,32 +153,35 @@
         def _():
             pass_prefix(t).wait_recv()
 
-        before = pr[t].astype(F32)
-        other = xr[t].astype(F32)
-        mine = loc[t]
+        before = pr[part(t)].astype(F32)
+        other = xr[part(t)].astype(F32)
+        mine = loc[part(t)]
 
         @pl.when(z < last)
         def _():
-            ps[t] = (before + (mine + other)).astype(link_t)
+            ps[part(t)] = (before + (mine + other)).astype(link_t)
             pass_prefix(t).start()
 
         @pl.when(core == 0)
         def _():
-            fs[t] = (before + mine).astype(BF16)
+            fs[part(t)] = (before + mine).astype(BF16)
             give_prefix(t).start()
-            pre[own0 + t] = before.astype(BF16)
+            pre[part(t, own0)] = before.astype(BF16)
 
         @pl.when(core == 1)
         def _():
-            fs[t] = before.astype(BF16)
+            fs[part(t)] = before.astype(BF16)
             give_prefix(t).start()
-            pre[own0 + t] = (before + other).astype(BF16)
+            pre[part(t, own0)] = (before + other).astype(BF16)
 
     @pl.when(z == 0)
     def _():
-        @pl.loop(0, HALF)
+        @pl.loop(0, PARTS)
         def _(t):
             prefix_chain(t)
+
+    for load in loads[4:]:
+        load.wait()
 
     rows = lax.broadcasted_iota(jnp.int32, (DIM, DIM), 0)
     cols = lax.broadcasted_iota(jnp.int32, (DIM, DIM), 1)
@@ -175,7 +207,7 @@
         return tn(q_ref[:, s], d)
 
     def norm_step(t):
-        remote(fs.at[t], pre.at[sib0 + t], f_sem, t, sib).wait_recv()
+        remote(fs.at[part(t)], pre.at[part(t, sib0)], f_sem, t, sib).wait_recv()
         other = through_norm(sib0 + t)
         mine = through_norm(own0 + t)
         ts[t] = other.astype(BF16)
@@ -189,26 +221,31 @@
         def _():
             pass_suffix(t).wait_recv()
 
-        after = rr[t].astype(F32)
-        other = tr[t].astype(F32)
-        mine = term[t]
+        after = rr[part(t)].astype(F32)
+        other = tr[part(t)].astype(F32)
+        mine = term[part(t)]
 
         @pl.when(z > 0)
         def _():
-            rs[t] = (after + (mine + other)).astype(link_t)
+            rs[part(t)] = (after + (mine + other)).astype(link_t)
             pass_suffix(t).start()
 
         @pl.when(core == 0)
         def _():
-            ss[t] = after.astype(BF16)
+            ss[part(t)] = after.astype(BF16)
             give_suffix(t).start()
-            suf[own0 + t] = (after + other).astype(BF16)
+            suf[part(t, own0)] = (after + other).astype(BF16)
 
         @pl.when(core == 1)
         def _():
-            ss[t] = (after + mine).astype(BF16)
+            ss[part(t)] = (after + mine).astype(BF16)
             give_suffix(t).start()
-            suf[own0 + t] = after.astype(BF16)
+            suf[part(t, own0)] = after.astype(BF16)
+
+    def store(i, h):
+        src, dst = ((qg_ref, qg_hbm), (kg_ref, kg_hbm), (vg_ref, vg_hbm))[i]
+        s = lanes(h)
+        return pltpu.make_async_copy(src.at[:, s], dst.at[:, s], out_sem.at[i, h])
 
     def within_block(h):
         s = lanes(h)
@@ -269,55 +306,81 @@
             gout[ctx] = jnp.sum(g2[...], axis=0) / jnp.sqrt(F32(tokens))
             others(n_ctx, ctx, lambda c: to_all(c).start())
 
-    chain_lag = jnp.minimum(2 + HALF * (last - z), 2 * HALF + 1)
-    finish_lag = jnp.maximum(chain_lag, HALF + 1) + 1
-
-    @pl.loop(0, 3 * HALF + 2)
+    chain_lag = jnp.minimum(
+        NORM_LAG + CHAIN_LAG + PARTS * (last - z), 2 * PARTS + NORM_LAG)
+    within_lag = PARTS + NORM_LAG
+    finish_lag = jnp.maximum(chain_lag, within_lag) + FINISH_LAG
+
+    gain_step = chain_lag + PARTS - 1 - jnp.clip(last - z - 1, 0, 2)
+
+    @pl.loop(0, 3 * PARTS + NORM_LAG + CHAIN_LAG + FINISH_LAG)
     def _(t):
-        @pl.when((t < HALF) & (z > 0))
+        @pl.when((t < PARTS) & (z > 0))
         def _():
             prefix_chain(t)
 
-        @pl.when((t >= 1) & (t < HALF + 1))
-        def _():
-            norm_step(t - 1)
-
-        @pl.when(t == HALF)
+        @pl.when((t >= NORM_LAG) & (t < PARTS + NORM_LAG))
+        def _():
+            norm_step(t - NORM_LAG)
+
+        @pl.when(t == PARTS - 1 + NORM_LAG)
         def _():
             gain_first()
 
         c = t - chain_lag
 
-        @pl.when((c >= 0) & (c < HALF))
+        @pl.when((c >= 0) & (c < PARTS))
         def _():
             suffix_chain(c)
 
-        @pl.when(c == HALF - 1)
+        @pl.when(t == gain_step)
         def _():
             gain_second()
 
-        w = t - (HALF + 1)
-
-        @pl.when((w >= 0) & (w < HALF))
-        def _():
-            within_block(own0 + w)
-            within_block(sib0 + w)
+        @pl.when(t == gain_step + 2)
+        def _():
+            gain_third()
+
+        w = t - within_lag
+
+        @pl.when((w >= 0) & (w < PARTS))
+        def _():
+            for i in range(WIDE):
+                within_block(own0 + w * WIDE + i)
+                within_block(sib0 + w * WIDE + i)
+            for i in range(WIDE):
+                store(0, own0 + w * WIDE + i).start()
+                store(0, sib0 + w * WIDE + i).start()
 
         f = t - finish_lag
 
-        @pl.when((f >= 0) & (f < HALF))
-        def _():
-            remote(ss.at[f], suf.at[sib0 + f], s_sem, f, sib).wait_recv()
-            finish(own0 + f)
-            finish(sib0 + f)
-
-    gain_third()
+        @pl.when((f >= 0) & (f < PARTS))
+        def _():
+            remote(ss.at[part(f)], suf.at[part(f, sib0)], s_sem, f, sib).wait_recv()
+            for j in range(WIDE):
+                finish(own0 + f * WIDE + j)
+                finish(sib0 + f * WIDE + j)
+            for j in range(WIDE):
+                for i in (1, 2):
+                    store(i, own0 + f * WIDE + j).start()
+                    store(i, sib0 + f * WIDE + j).start()
+
     others(n_own, ctx, lambda o: gain_copy(
         gout.at[o], gout.at[o], g3s.at[o], g3r.at[o], {"context": o}).wait_recv())
     for h in range(HEADS):
         sg_ref[:, h * DIM:(h + 1) * DIM] = gout[h // per, h % per]
 
-    @pl.loop(0, HALF)
+    last_store = pltpu.make_async_copy(sg_ref, sg_hbm, in_sem.at[0])
+    last_store.start()
+
+    @pl.loop(0, HEADS)
+    def _(h):
+        for i in range(3):
+            store(i, h).wait()
+
+    last_store.wait()
+
+    @pl.loop(0, PARTS)
     def _(t):
         swap_local(t).wait_send()
         give_prefix(t).wait_send()
@@ -338,6 +401,23 @@
     def _():
         others(n_dp, dp, lambda d: across(d).wait_send())
         others(n_ctx, ctx, lambda c: to_all(c).wait_send())
+
+
+def write_out(*refs):
+    sources, targets, held, sems = refs[:4], refs[4:8], refs[8:12], refs[12]
+    cuts = [
+        (i, pl.ds(r * 32, 32), r) for r in range(4) for i in range(3)] + [(3, pl.ds(0, 1), 0)]
+    ins = [pltpu.make_async_copy(sources[i].at[r], held[i].at[r], sems.at[0, i, n])
+           for i, r, n in cuts]
+    outs = [pltpu.make_async_copy(held[i].at[r], targets[i].at[r], sems.at[1, i, n])
+            for i, r, n in cuts]
+    for copy in ins:
+        copy.start()
+    for load, save in zip(ins, outs):
+        load.wait()
+        save.start()
+    for copy in outs:
+        copy.wait()
 
 
 def shards(n_dp, n_ctx, queries, keys, values, gain, out_grad):
@@ -348,15 +428,18 @@
     per = HEADS // n_own
     flat = lambda x: x.reshape(count, width)
     tile = lambda n, t: pltpu.VMEM((n, DIM, DIM), t)
-    vmem = pl.BlockSpec(memory_space=pltpu.VMEM)
+    hbm = pl.BlockSpec(memory_space=pltpu.HBM)
     dma = pltpu.SemaphoreType.DMA
     outs = pl.pallas_call(
         functools.partial(kernel, n_dp, n_ctx, tokens, link_t),
         out_shape=[jax.ShapeDtypeStruct((count, width), BF16)] * 3
         + [jax.ShapeDtypeStruct((1, width), F32)],
-        in_specs=[vmem] * 5,
-        out_specs=[vmem] * 4,
+        in_specs=[hbm] * 5,
+        out_specs=[hbm] * 4,
         scratch_shapes=[
+            *[pltpu.VMEM((count, width), BF16)] * 3,
+            pltpu.VMEM((1, width), F32), pltpu.VMEM((count, width), BF16),
+            *[pltpu.VMEM((count, width), BF16)] * 3, pltpu.VMEM((1, width), F32),
             tile(HALF, F32), tile(HALF, BF16), tile(HALF, BF16),
             tile(HALF, link_t), tile(HALF, link_t), tile(HALF, BF16), tile(HEADS, BF16),
             tile(HEADS, BF16), tile(HEADS, BF16),
@@ -368,14 +451,24 @@
             pltpu.VMEM((n_dp, per, 1, DIM), F32),
             pltpu.VMEM((n_own, per, 1, DIM), F32),
         ]
-        + [dma((2, HALF))] * 6
-        + [dma((n_own,)), dma((n_ctx,)), dma((n_dp,)), dma((n_dp,)), dma((n_ctx,)), dma((n_own,))],
+        + [dma((2, PARTS))] * 6
+        + [dma((n_own,)), dma((n_ctx,)), dma((n_dp,)), dma((n_dp,)), dma((n_ctx,)), dma((n_own,)),
+           dma((7,)), dma((3, HEADS))],
         compiler_params=pltpu.CompilerParams(
-            collective_id=0, has_side_effects=True, vmem_limit_bytes=40 * 2**20),
+            collective_id=0, has_side_effects=True, vmem_limit_bytes=60 * 2**20),
         cost_estimate=pl.CostEstimate(
             flops=24 * HEADS * DIM**3, bytes_accessed=7 * 2 * count * width,
             transcendentals=HEADS * DIM),
     )(flat(queries), flat(keys), flat(values), gain.reshape(1, width), flat(out_grad))
+    outs = pl.pallas_call(
+        write_out,
+        out_shape=[jax.ShapeDtypeStruct(x.shape, x.dtype) for x in outs],
+        in_specs=[hbm] * 4,
+        out_specs=[hbm] * 4,
+        scratch_shapes=[*[pltpu.VMEM((count, width), BF16)] * 3, pltpu.VMEM((1, width), F32),
+                        dma((2, 4, 4))],
+        compiler_params=pltpu.CompilerParams(vmem_limit_bytes=60 * 2**20),
+    )(*outs)
     shape = (1, count, width)
     return (outs[0].reshape(shape), outs[1].reshape(shape), outs[2].reshape(shape),
             outs[3].reshape(width))

time: 48.4 us -> 42.2 us (0.87)
  local copies, waits for them, and re-layouts: 7.83 us -> 0 us
  Pallas kernels: 39.6 us -> 41.3 us
    unnamed x14 -> x0, local copies, waits for them, and re-layouts: 7.83 us -> none
    pallas_call x0 -> x1, Pallas kernels: none -> 2.4 us  [shards(): pl.pallas_call(write_out, out_shape=[jax.ShapeDtypeStruct(x.shape, x.dtyp...]
    pallas_call x1, Pallas kernels: 39.6 us -> 38.9 us  [shards(): pl.pallas_call(functools.partial(kernel, n_dp, n_ctx, tokens, link_t), ou...]
where the time goes in v2:
time: 42.2 us; the launch traced here: 42 us
  Pallas kernels  41.3 us (98%)
  between operations  0.64 us (2%)
    pallas_call x1, Pallas kernels, shards(): pl.pallas_call(functools.partial(kernel, n_dp, n_ctx, tokens, link_t), ou...  38.9 us
    pallas_call x1, Pallas kernels, shards(): pl.pallas_call(write_out, out_shape=[jax.ShapeDtypeStruct(x.shape, x.dtyp...  2.4 us

profile of v2, /device:TPU:0, one launch (start us, length us, event | category | flops | bytes accessed | tf_op | source)
XLA Modules:
  0.0 42.0 jit_solution(16049277667379033641)
XLA Ops:
  0.6 38.9 %shard_map.84 = (bf16[128,2048]{1,0:T(8,128)(2,1)}, bf16[128,2048]{1,0:T(8,128)(2,1)}, bf16[128,2048]{1,0:T(8,128)(2,1)}, f32[1,2048]{1,0:T(1,128)}) custom-call(bf16[128,2048]{1,0:T(8,128)(2,1)} %bitcast.9, bf16[128,2048]{1,0:T(8,128)(2,1)} %bitcast.10, bf16[128,2048]{1,0:T(8,128)(2,1)} %bitcast.11, f32[1,2048]{1,0:T(1,128)} %bitcast.16, ...), custom_call_target="tpu_custom_call" | custom-call | flops 805306368 | bytes 3670016 | tf_op jit(solution)/shard_map/pallas_call | solution.py:433
  39.6 2.4 %shard_map.85 = (bf16[128,2048]{1,0:T(8,128)(2,1)}, bf16[128,2048]{1,0:T(8,128)(2,1)}, bf16[128,2048]{1,0:T(8,128)(2,1)}, f32[1,2048]{1,0:T(1,128)}) custom-call(bf16[128,2048]{1,0:T(8,128)(2,1)} %get-tuple-element.12.refs_0_, bf16[128,2048]{1,0:T(8,128)(2,1)} %get-tuple-element.13.refs_1_, bf16[128,2048]{1,0:T(8,128)(2,1)} %get-tuple-element.14.refs_2_, ...), custom_call_target="tpu_custom_call" | custom-call | tf_op jit(solution)/shard_map/pallas_call | solution.py:463

commit v3 on v1

v3 whole, which is shorter than its diff:
```python
import functools
import math

import jax
import jax.numpy as jnp
from jax import lax
from jax.experimental import pallas as pl
from jax.experimental.pallas import tpu as pltpu
from jax.sharding import PartitionSpec as P

HEADS = 16
HALF = HEADS // 2
DIM = 128
F32 = jnp.float32
BF16 = jnp.bfloat16
MESH = pl.DeviceIdType.MESH


def nn(a, b):
    return lax.dot_general(a, b, (((1,), (0,)), ((), ())), preferred_element_type=F32)


def nt(a, b):
    return lax.dot_general(a, b, (((1,), (1,)), ((), ())), preferred_element_type=F32)


def tn(a, b):
    return lax.dot_general(a, b, (((0,), (0,)), ((), ())), preferred_element_type=F32)


def kernel(
    n_dp, n_ctx, tokens, link_t,
    q_hbm, k_hbm, v_hbm, gain_hbm, dy_hbm,
    qg_hbm, kg_hbm, vg_hbm, sg_hbm,
    q_ref, k_ref, v_ref, dy_ref, gain_ref, qg_ref, kg_ref, vg_ref, sg_ref,
    loc, ps, pr, pre, attn, du, term, rs, rr, suf, kp, vp,
    gloc, g1, g2, gout,
    in_sem, gain_sem, swap_s, swap_r, out_sem, back_s, back_r,
    p_sem, r_sem, g1s, g1r, g2s, g2r, g3s, g3r,
):
    dp = lax.axis_index("dp")
    ctx = lax.axis_index("context")
    chips = n_ctx // 2
    last = chips - 1
    z = ctx // 2
    core = ctx % 2
    sib = z * 2 + (1 - core)
    own0 = core * HALF
    sib0 = (1 - core) * HALF
    per = gout.shape[1]
    n_own = gout.shape[0]
    side = n_own // 2

    def lanes(h):
        return pl.ds(pl.multiple_of(h * DIM, DIM), DIM)

    def half(h):
        return pl.ds(pl.multiple_of(h * DIM, DIM), HALF * DIM)

    pairs = ((k_hbm, k_ref), (v_hbm, v_ref), (q_hbm, q_ref), (dy_hbm, dy_ref))
    loads = [
        pltpu.make_async_copy(src.at[:, half(own0)], dst.at[core], in_sem.at[i])
        for i, (src, dst) in enumerate(pairs)]
    load_gain = pltpu.make_async_copy(gain_hbm.at[:, half(own0)], gain_ref, gain_sem.at[0])
    for load in loads:
        load.start()
    load_gain.start()

    barrier = pltpu.get_barrier_semaphore()

    def others(n, me, f):
        @pl.loop(0, n)
        def _(i):
            @pl.when(i != me)
            def _():
                f(i)

    others(n_ctx, ctx, lambda c: pl.semaphore_signal(
        barrier, inc=1, device_id={"context": c}, device_id_type=MESH))
    others(n_dp, dp, lambda d: pl.semaphore_signal(
        barrier, inc=1, device_id={"dp": d}, device_id_type=MESH))
    pl.semaphore_wait(barrier, n_ctx - 1 + n_dp - 1)

    def copy_to(src, dst, send, recv, device):
        return pltpu.make_async_remote_copy(
            src_ref=src, dst_ref=dst, send_sem=send, recv_sem=recv,
            device_id=device, device_id_type=MESH,
        )

    swaps = [
        copy_to(src.at[:, half(sib0)], dst.at[core], swap_s.at[i], swap_r.at[i], {"context": sib})
        for i, (src, dst) in enumerate(pairs)]
    arrivals = [
        copy_to(src.at[:, half(sib0)], dst.at[1 - core], swap_s.at[i], swap_r.at[i],
                {"context": sib})
        for i, (src, dst) in enumerate(pairs)]
    for swap in swaps:
        swap.start()

    def local_states(b):
        @pl.loop(0, HALF // 4)
        def _(i):
            for j in range(4):
                t = i * 4 + j
                s = lanes(t)
                loc[b, t] = tn(k_ref[b, :, s], v_ref[b, :, s])

    loads[0].wait()
    loads[1].wait()
    local_states(core)

    @pl.when(z == 0)
    def _():
        pr[...] = jnp.zeros_like(pr)

    @pl.when(z == last)
    def _():
        rr[...] = jnp.zeros_like(rr)

    arrivals[0].wait_recv()
    arrivals[1].wait_recv()
    local_states(1 - core)

    def pass_prefix(t):
        return copy_to(ps.at[t], pr.at[t], p_sem.at[0, t], p_sem.at[1, t],
                       {"context": jnp.minimum(ctx + 2, n_ctx - 2 + core)})

    def pass_suffix(t):
        return copy_to(rs.at[t], rr.at[t], r_sem.at[0, t], r_sem.at[1, t],
                       {"context": jnp.maximum(ctx - 2, core)})

    def prefix_chain(t):
        @pl.when(z > 0)
        def _():
            pass_prefix(t).wait_recv()

        before = pr[t].astype(F32)

        @pl.when(z < last)
        def _():
            ps[t] = (before + (loc[0, t] + loc[1, t])).astype(link_t)
            pass_prefix(t).start()

        pre[0, t] = before.astype(BF16)
        pre[1, t] = (before + loc[0, t]).astype(BF16)

    @pl.when(z == 0)
    def _():
        @pl.loop(0, HALF)
        def _(t):
            prefix_chain(t)

    for load in (*loads[2:], load_gain):
        load.wait()
    for arrival in arrivals[2:]:
        arrival.wait_recv()

    rows = lax.broadcasted_iota(jnp.int32, (DIM, DIM), 0)
    cols = lax.broadcasted_iota(jnp.int32, (DIM, DIM), 1)

    @pl.loop(0, HALF // 2)
    def _(i):
        for j in range(2):
            t = i * 2 + j
            s = lanes(t)
            for b in range(2):
                attn[b, t] = jnp.where(
                    rows >= cols, nt(q_ref[b, :, s], k_ref[b, :, s]), 0.0).astype(BF16)

    def norm_step(t):
        s = lanes(t)
        part = []
        for b in range(2):
            u = nn(q_ref[b, :, s], pre[b, t]) + nn(attn[b, t], v_ref[b, :, s])
            inv = lax.rsqrt(jnp.mean(u * u, axis=-1, keepdims=True) + 1e-6)
            unit = u * inv
            grad = dy_ref[b, :, s].astype(F32)
            part.append(jnp.sum(grad * unit, axis=0, keepdims=True))
            scaled = gain_ref[:, s] * grad
            d = (scaled - unit * jnp.mean(scaled * unit, axis=-1, keepdims=True)) * inv
            d = d.astype(BF16)
            du[b, t] = d
            term[b, t] = tn(q_ref[b, :, s], d)
        gloc[t] = part[0] + part[1]

    def suffix_chain(t):
        @pl.when(z < last)
        def _():
            pass_suffix(t).wait_recv()

        after = rr[t].astype(F32)

        @pl.when(z > 0)
        def _():
            rs[t] = (after + (term[0, t] + term[1, t])).astype(link_t)
            pass_suffix(t).start()

        suf[1, t] = after.astype(BF16)
        suf[0, t] = (after + term[1, t]).astype(BF16)

    results = ((qg_ref, qg_hbm), (kg_ref, kg_hbm), (vg_ref, vg_hbm))

    def store(i, t):
        src, dst = results[i]
        return pltpu.make_async_copy(
            src.at[core, :, lanes(t)], dst.at[:, lanes(own0 + t)], out_sem.at[i, t])

    def give_back(i, t, first):
        src, dst = results[i]
        return copy_to(src.at[1 - core, :, lanes(t)], dst.at[:, lanes(first + t)],
                       back_s.at[i, t], back_r.at[i, t], {"context": sib})

    def within_block(t):
        s = lanes(t)
        for b in range(2):
            d = du[b, t]
            da = jnp.where(rows >= cols, nt(d, v_ref[b, :, s]), 0.0).astype(BF16)
            qg_ref[b, :, s] = (nt(d, pre[b, t]) + nn(da, k_ref[b, :, s])).astype(BF16)
            kp[b, t] = tn(da, q_ref[b, :, s])
            vp[b, t] = tn(attn[b, t], d)
        give_back(0, t, own0).start()
        store(0, t).start()

    def finish(t):
        s = lanes(t)
        for b in range(2):
            kg_ref[b, :, s] = (kp[b, t] + nt(v_ref[b, :, s], suf[b, t])).astype(BF16)
            vg_ref[b, :, s] = (vp[b, t] + nn(k_ref[b, :, s], suf[b, t])).astype(BF16)
        for i in (1, 2):
            give_back(i, t, own0).start()
        for i in (1, 2):
            store(i, t).start()

    def to_owner(i):
        return copy_to(gloc.at[pl.ds(i * per, per)], g1.at[z], g1s.at[i], g1r.at[z],
                       {"context": core * side + i})

    def across(d):
        return copy_to(g2.at[dp], g2.at[dp], g2s.at[d], g2r.at[dp], {"dp": d})

    def to_all(c):
        return copy_to(gout.at[ctx], gout.at[ctx], g3s.at[c], g3r.at[ctx], {"context": c})

    mine = ctx - core * side

    def gain_first():
        others(side, mine, lambda i: to_owner(i).start())

        @pl.when((mine >= 0) & (mine < side))
        def _():
            g1[z] = gloc[pl.ds(mine * per, per)]

    def gain_second():
        @pl.when(ctx < n_own)
        def _():
            @pl.loop(0, chips)
            def _(c):
                @pl.when(2 * c + ctx // side != ctx)
                def _():
                    copy_to(gloc.at[pl.ds(0, per)], g1.at[c], g1s.at[0], g1r.at[c],
                            {"context": 2 * c + ctx // side}).wait_recv()

            g2[dp] = jnp.sum(g1[...], axis=0)
            others(n_dp, dp, lambda d: across(d).start())

    def gain_third():
        @pl.when(ctx < n_own)
        def _():
            others(n_dp, dp, lambda d: copy_to(
                g2.at[d], g2.at[d], g2s.at[d], g2r.at[d], {"dp": d}).wait_recv())
            gout[ctx] = jnp.sum(g2[...], axis=0) / jnp.sqrt(F32(tokens))
            others(n_ctx, ctx, lambda c: to_all(c).start())

    chain_lag = jnp.where(
        z == last, 0, jnp.minimum(HALF * (last - z) + 2, 2 * HALF))
    finish_lag = jnp.maximum(chain_lag, HALF)
    gain_step = chain_lag + HALF - 1 - jnp.clip(2 * (last - z - 1), 0, 4)

    @pl.loop(0, 3 * HALF + 3)
    def _(t):
        @pl.when((t < HALF) & (z > 0))
        def _():
            prefix_chain(t)

        @pl.when(t < HALF)
        def _():
            norm_step(t)

        @pl.when(t == HALF - 1)
        def _():
            gain_first()

        c = t - chain_lag

        @pl.when((c >= 0) & (c < HALF))
        def _():
            suffix_chain(c)

        @pl.when(t == gain_step)
        def _():
            gain_second()

        @pl.when(t == gain_step + 2)
        def _():
            gain_third()

        w = t - HALF

        @pl.when((w >= 0) & (w < HALF))
        def _():
            within_block(w)

        f = t - finish_lag

        @pl.when((f >= 0) & (f < HALF))
        def _():
            finish(f)

    others(n_own, ctx, lambda o: copy_to(
        gout.at[o], gout.at[o], g3s.at[o], g3r.at[o], {"context": o}).wait_recv())
    for h in range(HEADS):
        sg_ref[:, h * DIM:(h + 1) * DIM] = gout[h // per, h % per]
    last_store = pltpu.make_async_copy(sg_ref, sg_hbm, gain_sem.at[0])
    last_store.start()

    @pl.loop(0, HALF)
    def _(t):
        for i in range(3):
            store(i, t).wait()
            give_back(i, t, own0).wait_send()
            give_back(i, t, sib0).wait_recv()

        @pl.when(z < last)
        def _():
            pass_prefix(t).wait_send()

        @pl.when(z > 0)
        def _():
            pass_suffix(t).wait_send()

    for swap in swaps:
        swap.wait_send()
    others(side, mine, lambda i: to_owner(i).wait_send())

    @pl.when(ctx < n_own)
    def _():
        others(n_dp, dp, lambda d: across(d).wait_send())
        others(n_ctx, ctx, lambda c: to_all(c).wait_send())

    last_store.wait()


def write_out(*refs):
    sources, targets, held, sems = refs[:4], refs[4:8], refs[8:12], refs[12]
    cuts = [
        (i, pl.ds(r * 32, 32), r) for r in range(4) for i in range(3)] + [(3, pl.ds(0, 1), 0)]
    ins = [pltpu.make_async_copy(sources[i].at[r], held[i].at[r], sems.at[0, i, n])
           for i, r, n in cuts]
    outs = [pltpu.make_async_copy(held[i].at[r], targets[i].at[r], sems.at[1, i, n])
            for i, r, n in cuts]
    for copy in ins:
        copy.start()
    for load, save in zip(ins, outs):
        load.wait()
        save.start()
    for copy in outs:
        copy.wait()


def shards(n_dp, n_ctx, queries, keys, values, gain, out_grad):
    count, width = queries.shape[1:]
    tokens = queries.shape[0] * n_dp * count * n_ctx
    link_t = BF16 if n_ctx <= 16 else F32
    n_own = min(n_ctx, HEADS)
    per = HEADS // n_own
    flat = lambda x: x.reshape(count, width)
    tile = lambda t: pltpu.VMEM((2, HALF, DIM, DIM), t)
    hbm = pl.BlockSpec(memory_space=pltpu.HBM)
    dma = pltpu.SemaphoreType.DMA
    outs = pl.pallas_call(
        functools.partial(kernel, n_dp, n_ctx, tokens, link_t),
        out_shape=[jax.ShapeDtypeStruct((count, width), BF16)] * 3
        + [jax.ShapeDtypeStruct((1, width), F32)],
        in_specs=[hbm] * 5,
        out_specs=[hbm] * 4,
        scratch_shapes=[
            *[pltpu.VMEM((2, count, width // 2), BF16)] * 4, pltpu.VMEM((1, width // 2), F32),
            *[pltpu.VMEM((2, count, width // 2), BF16)] * 3, pltpu.VMEM((1, width), F32),
            tile(F32), pltpu.VMEM((HALF, DIM, DIM), link_t), pltpu.VMEM((HALF, DIM, DIM), link_t),
            tile(BF16), tile(BF16), tile(BF16), tile(F32),
            pltpu.VMEM((HALF, DIM, DIM), link_t), pltpu.VMEM((HALF, DIM, DIM), link_t),
            tile(BF16), tile(F32), tile(F32),
            pltpu.VMEM((HALF, 1, DIM), F32),
            pltpu.VMEM((n_ctx // 2, per, 1, DIM), F32),
            pltpu.VMEM((n_dp, per, 1, DIM), F32),
            pltpu.VMEM((n_own, per, 1, DIM), F32),
            dma((4,)), dma((1,)), dma((4,)), dma((4,)), *[dma((3, HALF))] * 3,
            dma((2, HALF)), dma((2, HALF)), dma((n_own // 2,)), dma((n_ctx // 2,)),
            dma((n_dp,)), dma((n_dp,)), dma((n_ctx,)), dma((n_own,)),
        ],
        compiler_params=pltpu.CompilerParams(
            collective_id=0, has_side_effects=True, vmem_limit_bytes=60 * 2**20),
        cost_estimate=pl.CostEstimate(
            flops=24 * HEADS * DIM**3, bytes_accessed=7 * 2 * count * width,
            transcendentals=HEADS * DIM),
    )(flat(queries), flat(keys), flat(values), gain.reshape(1, width), flat(out_grad))
    outs = pl.pallas_call(
        write_out,
        out_shape=[jax.ShapeDtypeStruct(x.shape, x.dtype) for x in outs],
        in_specs=[hbm] * 4,
        out_specs=[hbm] * 4,
        scratch_shapes=[*[pltpu.VMEM((count, width), BF16)] * 3, pltpu.VMEM((1, width), F32),
                        dma((2, 4, 4))],
        compiler_params=pltpu.CompilerParams(vmem_limit_bytes=60 * 2**20),
    )(*outs)
    shape = (1, count, width)
    return (outs[0].reshape(shape), outs[1].reshape(shape), outs[2].reshape(shape),
            outs[3].reshape(width))


def solution(mesh):
    rows = P("dp", "context", None)
    return jax.shard_map(
        functools.partial(shards, mesh.shape["dp"], mesh.shape["context"]),
        mesh=mesh,
        in_specs=(rows, rows, rows, P(), rows),
        out_specs=(rows, rows, rows, P()),
        check_vma=False,
    )
```

time: 48.4 us -> 41.2 us (0.85)
  local copies, waits for them, and re-layouts: 7.83 us -> 0 us
  Pallas kernels: 39.6 us -> 40.4 us
    unnamed x14 -> x0, local copies, waits for them, and re-layouts: 7.83 us -> none
    pallas_call x0 -> x1, Pallas kernels: none -> 2.4 us  [shards(): pl.pallas_call(write_out, out_shape=[jax.ShapeDtypeStruct(x.shape, x.dtyp...]
    pallas_call x1, Pallas kernels: 39.6 us -> 38 us  [shards(): pl.pallas_call(functools.partial(kernel, n_dp, n_ctx, tokens, link_t), ou...]
where the time goes in v3:
time: 41.2 us; the launch traced here: 41 us
  Pallas kernels  40.4 us (98%)
  between operations  0.64 us (2%)
    pallas_call x1, Pallas kernels, shards(): pl.pallas_call(functools.partial(kernel, n_dp, n_ctx, tokens, link_t), ou...  38 us
    pallas_call x1, Pallas kernels, shards(): pl.pallas_call(write_out, out_shape=[jax.ShapeDtypeStruct(x.shape, x.dtyp...  2.4 us

profile of v3, /device:TPU:0, one launch (start us, length us, event | category | flops | bytes accessed | tf_op | source)
XLA Modules:
  0.0 41.0 jit_solution(119483116909264927)
XLA Ops:
  0.6 38.0 %shard_map.84 = (bf16[128,2048]{1,0:T(8,128)(2,1)}, bf16[128,2048]{1,0:T(8,128)(2,1)}, bf16[128,2048]{1,0:T(8,128)(2,1)}, f32[1,2048]{1,0:T(1,128)}) custom-call(bf16[128,2048]{1,0:T(8,128)(2,1)} %bitcast.9, bf16[128,2048]{1,0:T(8,128)(2,1)} %bitcast.10, bf16[128,2048]{1,0:T(8,128)(2,1)} %bitcast.11, f32[1,2048]{1,0:T(1,128)} %bitcast.16, ...), custom_call_target="tpu_custom_call" | custom-call | flops 805306368 | bytes 3670016 | tf_op jit(solution)/shard_map/pallas_call | solution.py:380
  38.6 2.4 %shard_map.85 = (bf16[128,2048]{1,0:T(8,128)(2,1)}, bf16[128,2048]{1,0:T(8,128)(2,1)}, bf16[128,2048]{1,0:T(8,128)(2,1)}, f32[1,2048]{1,0:T(1,128)}) custom-call(bf16[128,2048]{1,0:T(8,128)(2,1)} %get-tuple-element.12.refs_0_, bf16[128,2048]{1,0:T(8,128)(2,1)} %get-tuple-element.13.refs_1_, bf16[128,2048]{1,0:T(8,128)(2,1)} %get-tuple-element.14.refs_2_, ...), custom_call_target="tpu_custom_call" | custom-call | tf_op jit(solution)/shard_map/pallas_call | solution.py:407
